TPU v7x, 32 devices: a whole 2x2x4 slice. The times are simulated.
32 devices in a mesh: ep: 8 (over z, y), tp: 4 (over x, core).
Axes of the slice: x: 2, y: 2, z: 4, core: 2. Of those that a mesh axis runs over, the one named last changes fastest.
Arguments:
- tokens: bfloat16 [1024, 2048], P('ep', 'tp'), may hold values from -6 to 6
- cotangent: bfloat16 [1024, 2048], P('ep', 'tp'), may hold values from -6 to 6
- token_expert: int32 [1024], P('ep'), may hold values from 0 to 7, as said below
- partner: int32 [8], replicated, may hold values from 0 to 7, as said below
- gate_weight: bfloat16 [8, 768, 2048], P('ep', 'tp'), may hold values from -0.125 to 0.125
- up_weight: bfloat16 [8, 768, 2048], P('ep', 'tp'), may hold values from -0.125 to 0.125
- down_weight: bfloat16 [8, 768, 2048], P('ep', 'tp'), may hold values from -0.21875 to 0.21875
Outputs:
- token_grad: bfloat16 [1024, 2048], P('ep', 'tp')
- gate_grad: bfloat16 [8, 768, 2048], P('ep', 'tp')
- up_grad: bfloat16 [8, 768, 2048], P('ep', 'tp')
- down_grad: bfloat16 [8, 768, 2048], P('ep', 'tp')
Inputs may be any that keep to these rules, and one draw needn't show every extreme that they name: partner[partner[d]] = d and partner[d] != d: the devices of ep swap their experts in pairs. `token_expert`: each aligned block of 128 rows (the rows of one device) names each expert at most 32 times, and one expert, the same for all blocks, exactly 32 times in every block.
All inputs are finite; a program needn't handle non-finite values.
Results may differ from a plain program's by a relative error of at most 0.0049.
Values may be sent and summed in bfloat16 or wider, within the bound.
A program may use at most 64 MiB of HBM per device.

v0:
```python
import functools

import jax
import jax.numpy as jnp
from jax import lax
from jax.experimental import pallas as pl
from jax.experimental.pallas import tpu as pltpu
from jax.sharding import PartitionSpec as P

F32 = jnp.float32
BF16 = jnp.bfloat16


def contract_last(left, right):
    return lax.dot_general(left, right, (((1,), (1,)), ((), ())), preferred_element_type=F32)


def contract_first(left, right):
    return lax.dot_general(left, right, (((0,), (0,)), ((), ())), preferred_element_type=F32)


def expert_terms(gate, upward, hidden_grad):
    sigmoid_gate = jax.nn.sigmoid(gate)
    activated = gate * sigmoid_gate
    hidden = (activated * upward).astype(BF16)
    up_term = (hidden_grad * activated).astype(BF16)
    gate_term = (hidden_grad * upward * sigmoid_gate * (1.0 + gate * (1.0 - sigmoid_gate))).astype(BF16)
    return gate_term, up_term, hidden


def capacity_of(rows, devices):
    return max(2, (2 * rows + devices - 1) // devices)


def relocate(arrays, partner):
    devices = lax.axis_size("ep")
    pieces = tuple((matrix.reshape(devices, -1) for matrix in arrays))
    spread = lax.all_to_all(pieces, "ep", split_axis=0, concat_axis=0, tiled=True)
    chosen = tuple((jnp.take(piece, partner, axis=0) for piece in spread))
    returned = lax.all_to_all(chosen, "ep", split_axis=0, concat_axis=0, tiled=True)
    return tuple((piece.reshape(matrix.shape) for piece, matrix in zip(returned, arrays)))


def plain_body(tokens, cotangent, token_expert, partner, gate_weight, up_weight, down_weight):
    devices = lax.axis_size("ep")
    row_count = tokens.shape[0]
    capacity = capacity_of(row_count, devices)
    gate_weight, up_weight, down_weight = relocate((gate_weight, up_weight, down_weight), partner)
    owners = jnp.take(partner, token_expert, axis=0)
    same_owner = owners[:, None] == owners[None, :]
    earlier = jnp.arange(row_count)[:, None] > jnp.arange(row_count)[None, :]
    position = jnp.sum((same_owner & earlier).astype(jnp.int32), axis=1)
    slot_of = owners * capacity + position
    one_hot = (slot_of[None, :] == jnp.arange(devices * capacity)[:, None]).astype(BF16)
    send_x = jnp.dot(one_hot, tokens, preferred_element_type=F32).astype(BF16)
    send_g = jnp.dot(one_hot, cotangent, preferred_element_type=F32).astype(BF16)
    received_x = lax.all_to_all(send_x, "ep", split_axis=0, concat_axis=0, tiled=True)
    received_g = lax.all_to_all(send_g, "ep", split_axis=0, concat_axis=0, tiled=True)
    full_x = lax.all_gather(received_x, "tp", axis=1, tiled=True)
    full_g = lax.all_gather(received_g, "tp", axis=1, tiled=True)
    w_gate, w_up, w_down = gate_weight[0], up_weight[0], down_weight[0]
    gate_term, up_term, hidden = expert_terms(
        contract_last(full_x, w_gate), contract_last(full_x, w_up), contract_last(full_g, w_down)
    )
    partial_value = jnp.dot(gate_term, w_gate, preferred_element_type=F32) + jnp.dot(
        up_term, w_up, preferred_element_type=F32
    )
    grad_gate = contract_first(gate_term, full_x).astype(BF16)[None]
    grad_up = contract_first(up_term, full_x).astype(BF16)[None]
    grad_down = contract_first(hidden, full_g).astype(BF16)[None]
    share = lax.psum_scatter(partial_value, "tp", scatter_dimension=1, tiled=True).astype(BF16)
    coming_back = lax.all_to_all(share, "ep", split_axis=0, concat_axis=0, tiled=True)
    token_grad = contract_first(one_hot, coming_back).astype(BF16)
    return (token_grad, grad_gate, grad_up, grad_down)


def remote(src, dst, send, recv, device):
    return pltpu.make_async_remote_copy(
        src_ref=src, dst_ref=dst, send_sem=send, recv_sem=recv,
        device_id=device, device_id_type=pl.DeviceIdType.MESH,
    )


def swap_kernel(
    n, cap, groups,
    partner, te, tok, cot, wg_in, wu_in, wd_in,
    tg_out, gg_out, gu_out, gd_out,
    w_v, send_e, send_p, full_e, full_p, terms, mid, send2, terms_p,
    keep, c1s, c1r, c2s, c2r, shares, ret,
    w_sem, ae, ap, be, bp, e1, e2, c1, c2, dd,
):
    rows, width = tok.shape
    units = wg_in.shape[1]
    per = n // groups
    me = lax.axis_index("ep")
    t = lax.axis_index("tp")
    sib = t + 1 - 2 * lax.rem(t, 2)
    ctr = lax.rem(t + 2, 4)
    far = lax.rem(sib + 2, 4)
    ahead = lambda k: lax.rem(me + k, n)
    behind = lambda k: lax.rem(me + n - k, n)

    barrier = pltpu.get_barrier_semaphore()

    def greet(k, carry):
        pl.semaphore_signal(barrier, inc=1, device_id={"ep": ahead(k)}, device_id_type=pl.DeviceIdType.MESH)
        return carry

    lax.fori_loop(1, n, greet, 0)
    for other in (sib, ctr):
        pl.semaphore_signal(barrier, inc=1, device_id={"tp": other}, device_id_type=pl.DeviceIdType.MESH)

    w_copies = [
        pltpu.make_async_copy(
            w.at[0, :, pl.ds(q * width, width)], w_v.at[i, q], w_sem.at[i, q]
        )
        for i, w in enumerate((wg_in, wu_in, wd_in))
        for q in range(4)
    ]
    for copy in w_copies:
        copy.start()

    te_lane = jnp.broadcast_to(te[...].astype(F32), (rows, rows))
    te_sub = te_lane.T
    at0 = lax.broadcasted_iota(jnp.int32, (rows, rows), 0)
    at1 = lax.broadcasted_iota(jnp.int32, (rows, rows), 1)
    same = te_lane == te_sub
    pos_lane = jnp.sum(jnp.where(same & (at0 < at1), 1.0, 0.0), axis=0, keepdims=True)
    pos_sub = jnp.sum(jnp.where(same & (at1 < at0), 1.0, 0.0), axis=1, keepdims=True)
    slot_lane = te[...].astype(F32) * float(cap) + pos_lane
    slot_sub = te_sub[:, :1] * float(cap) + pos_sub
    slots = n * cap
    down = lax.broadcasted_iota(jnp.int32, (slots, rows), 0).astype(F32)
    across = lax.broadcasted_iota(jnp.int32, (rows, slots), 1).astype(F32)

    def pick(slot, send):
        hot = jnp.where(down == slot, 1.0, 0.0).astype(BF16)
        for i, source in enumerate((tok, cot)):
            rows_of = jnp.dot(hot, source[...], preferred_element_type=F32).astype(BF16)
            send[:, i] = rows_of.reshape(n, cap, width)

    def dispatch(send, full, sem):
        def go(k, carry):
            to = ahead(k)
            remote(send.at[to], full.at[t, me], sem.at[0, to], sem.at[1, me], {"ep": to}).start()
            return carry
        lax.fori_loop(1, n, go, 0)
        full[t, me] = send[me]

    def share_own(full, b, s):
        remote(full.at[t, s], full.at[t, s], b.at[1, s], b.at[4, s], {"tp": ctr}).start()
        remote(full.at[t, s], full.at[t, s], b.at[0, s], b.at[3, s], {"tp": sib}).start()

    def got_own(full, a, s, k):
        remote(full.at[t, s], full.at[t, s], a.at[0, s], a.at[1, s], {"ep": s}).wait_recv()

    def pass_on(full, b, s):
        remote(full.at[ctr, s], full.at[ctr, s], b.at[1, s], b.at[4, s], {"tp": ctr}).wait_recv()
        remote(full.at[ctr, s], full.at[ctr, s], b.at[2, s], b.at[5, s], {"tp": sib}).start()

    def got_sibling(full, b, s):
        remote(full.at[sib, s], full.at[sib, s], b.at[0, s], b.at[3, s], {"tp": sib}).wait_recv()
        remote(full.at[far, s], full.at[far, s], b.at[2, s], b.at[5, s], {"tp": sib}).wait_recv()

    def spread(full, a, b):
        share_own(full, b, me)

        def step(k, carry):
            s = behind(k)
            got_own(full, a, s, k)
            share_own(full, b, s)
            pass_on(full, b, behind(k - 1))
            return carry
        lax.fori_loop(1, n, step, 0)
        pass_on(full, b, behind(n - 1))

    pick(slot_lane, send_e)
    pl.semaphore_wait(barrier, n + 1)
    dispatch(send_e, full_e, ae)
    moved = pos_lane
    for e in range(n):
        moved = moved + jnp.where(te[...] == e, (partner[e] * cap).astype(F32), 0.0)
    pick(moved, send_p)
    spread(full_e, ae, be)
    dispatch(send_p, full_p, ap)
    for copy in w_copies:
        copy.wait()

    slices = (t, ctr, sib, far)
    for h in range(groups):
        ks = range(h * per, (h + 1) * per)
        for k in ks:
            got_sibling(full_e, be, behind(k))
        gate = jnp.zeros((per * cap, units), F32)
        upward = jnp.zeros((per * cap, units), F32)
        hidden_grad = jnp.zeros((per * cap, units), F32)
        for q in range(4):
            x_q = jnp.concatenate([full_e[q, behind(k), 0] for k in ks], axis=0)
            g_q = jnp.concatenate([full_e[q, behind(k), 1] for k in ks], axis=0)
            gate = gate + contract_last(x_q, w_v[0, q])
            upward = upward + contract_last(x_q, w_v[1, q])
            hidden_grad = hidden_grad + contract_last(g_q, w_v[2, q])
        gate_term, up_term, hidden = expert_terms(gate, upward, hidden_grad)
        for j, k in enumerate(ks):
            cut = slice(j * cap, (j + 1) * cap)
            terms[behind(k), :, 0:units] = gate_term[cut]
            terms[behind(k), :, units : 2 * units] = up_term[cut]
            terms[behind(k), :, 2 * units : 3 * units] = hidden[cut]
            if terms.shape[2] > 3 * units:
                terms[behind(k), :, 3 * units :] = jnp.zeros((cap, terms.shape[2] - 3 * units), BF16)
        for i in (2, 3):
            q = slices[i]
            c1s[h, i - 2] = (
                jnp.dot(gate_term, w_v[0, q], preferred_element_type=F32)
                + jnp.dot(up_term, w_v[1, q], preferred_element_type=F32)
            ).astype(BF16)
        remote(c1s.at[h], c1r.at[h], c1.at[0, h], c1.at[1, h], {"tp": sib}).start()
        for k in ks:
            s = behind(k)
            if k == 0:
                mid[me] = terms[me]
            else:
                remote(terms.at[s], mid.at[me], e1.at[0, s], e1.at[1, me], {"ep": s}).start()
        for i in (0, 1):
            q = slices[i]
            keep[h, i] = jnp.dot(gate_term, w_v[0, q], preferred_element_type=F32) + jnp.dot(
                up_term, w_v[1, q], preferred_element_type=F32
            )

    for h in range(groups):
        remote(c1s.at[h], c1r.at[h], c1.at[0, h], c1.at[1, h], {"tp": sib}).wait_recv()
        c2s[h] = (keep[h, 1] + c1r[h, 1].astype(F32)).astype(BF16)
        remote(c2s.at[h], c2r.at[h], c2.at[0, h], c2.at[1, h], {"tp": ctr}).start()

    def first_hop(k, carry):
        s = ahead(k)
        remote(mid.at[s], mid.at[s], e1.at[0, s], e1.at[1, s], {"ep": s}).wait_recv()
        return carry
    lax.fori_loop(1, n, first_hop, 0)

    for h in range(groups):
        remote(c2s.at[h], c2r.at[h], c2.at[0, h], c2.at[1, h], {"tp": ctr}).wait_recv()
        total = (keep[h, 0] + c1r[h, 0].astype(F32) + c2r[h].astype(F32)).astype(BF16)
        shares[h * per : (h + 1) * per] = total.reshape(per, cap, width)
        for k in range(h * per, (h + 1) * per):
            s = behind(k)
            if k == 0:
                ret[me] = shares[0]
            else:
                remote(shares.at[k], ret.at[me], dd.at[0, s], dd.at[1, me], {"ep": s}).start()

    def second_hop(k, carry):
        d = ahead(k)
        send2[d] = mid[partner[d]]
        remote(send2.at[d], terms_p.at[me], e2.at[0, d], e2.at[1, me], {"ep": d}).start()
        return carry
    lax.fori_loop(1, n, second_hop, 0)
    terms_p[me] = mid[partner[me]]

    spread(full_p, ap, bp)

    def returned(k, carry):
        s = behind(k)
        remote(ret.at[s], ret.at[s], dd.at[0, s], dd.at[1, s], {"ep": s}).wait_recv()
        return carry
    lax.fori_loop(1, n, returned, 0)
    home = jnp.where(across == slot_sub, 1.0, 0.0).astype(BF16)
    tg_out[...] = jnp.dot(home, ret[...].reshape(slots, width), preferred_element_type=F32).astype(BF16)

    def arrived(k, carry):
        s = behind(k)
        remote(terms_p.at[s], terms_p.at[s], e2.at[0, s], e2.at[1, s], {"ep": s}).wait_recv()
        return carry
    lax.fori_loop(1, n, arrived, 0)

    def gathered(k, carry):
        got_sibling(full_p, bp, behind(k))
        return carry
    lax.fori_loop(0, n, gathered, 0)

    flat = terms_p[...].reshape(slots, terms_p.shape[2])
    turned = flat.astype(F32).T.astype(BF16)
    for q in range(4):
        columns = slice(q * width, (q + 1) * width)
        x_q = full_p[q, :, 0].reshape(slots, width)
        g_q = full_p[q, :, 1].reshape(slots, width)
        gg_out[0, :, columns] = jnp.dot(turned[:units], x_q, preferred_element_type=F32).astype(BF16)
        gu_out[0, :, columns] = jnp.dot(turned[units : 2 * units], x_q, preferred_element_type=F32).astype(BF16)
        gd_out[0, :, columns] = jnp.dot(turned[2 * units : 3 * units], g_q, preferred_element_type=F32).astype(BF16)

    def drain(k, carry):
        s = ahead(k)
        remote(send_e.at[s], send_e.at[s], ae.at[0, s], ae.at[1, s], {"ep": s}).wait_send()
        remote(send_p.at[s], send_p.at[s], ap.at[0, s], ap.at[1, s], {"ep": s}).wait_send()
        remote(terms.at[s], terms.at[s], e1.at[0, s], e1.at[1, s], {"ep": s}).wait_send()
        remote(send2.at[s], send2.at[s], e2.at[0, s], e2.at[1, s], {"ep": s}).wait_send()
        remote(ret.at[s], ret.at[s], dd.at[0, s], dd.at[1, s], {"ep": s}).wait_send()
        return carry
    lax.fori_loop(1, n, drain, 0)

    def drain_tp(s, carry):
        for full, b in ((full_e, be), (full_p, bp)):
            for i, (q, other) in enumerate(((t, sib), (t, ctr), (ctr, sib))):
                remote(full.at[q, s], full.at[q, s], b.at[i, s], b.at[3 + i, s], {"tp": other}).wait_send()
        return carry
    lax.fori_loop(0, n, drain_tp, 0)
    for h in range(groups):
        remote(c1s.at[h], c1r.at[h], c1.at[0, h], c1.at[1, h], {"tp": sib}).wait_send()
        remote(c2s.at[h], c2r.at[h], c2.at[0, h], c2.at[1, h], {"tp": ctr}).wait_send()


def kernel_body(tokens, cotangent, token_expert, partner, gate_weight, up_weight, down_weight):
    n = lax.axis_size("ep")
    rows, width = tokens.shape
    _, units, features = gate_weight.shape
    cap = capacity_of(rows, n)
    groups = 2
    per = n // groups
    padded = -(-3 * units // 128) * 128
    dma = pltpu.SemaphoreType.DMA
    vmem = pl.BlockSpec(memory_space=pltpu.VMEM)
    anywhere = pl.BlockSpec(memory_space=pl.ANY)
    grad = jax.ShapeDtypeStruct((1, units, features), BF16)
    return pl.pallas_call(
        functools.partial(swap_kernel, n, cap, groups),
        out_shape=(jax.ShapeDtypeStruct((rows, width), BF16), grad, grad, grad),
        in_specs=[pl.BlockSpec(memory_space=pltpu.SMEM), vmem, vmem, vmem, anywhere, anywhere, anywhere],
        out_specs=(vmem, vmem, vmem, vmem),
        scratch_shapes=[
            pltpu.VMEM((3, 4, units, width), BF16),
            pltpu.VMEM((n, 2, cap, width), BF16),
            pltpu.VMEM((n, 2, cap, width), BF16),
            pltpu.VMEM((4, n, 2, cap, width), BF16),
            pltpu.VMEM((4, n, 2, cap, width), BF16),
            pltpu.VMEM((n, cap, padded), BF16),
            pltpu.VMEM((n, cap, padded), BF16),
            pltpu.VMEM((n, cap, padded), BF16),
            pltpu.VMEM((n, cap, padded), BF16),
            pltpu.VMEM((groups, 2, per * cap, width), F32),
            pltpu.VMEM((groups, 2, per * cap, width), BF16),
            pltpu.VMEM((groups, 2, per * cap, width), BF16),
            pltpu.VMEM((groups, per * cap, width), BF16),
            pltpu.VMEM((groups, per * cap, width), BF16),
            pltpu.VMEM((n, cap, width), BF16),
            pltpu.VMEM((n, cap, width), BF16),
            dma((3, 4)),
            dma((2, n)),
            dma((2, n)),
            dma((6, n)),
            dma((6, n)),
            dma((2, n)),
            dma((2, n)),
            dma((2, groups)),
            dma((2, groups)),
            dma((2, n)),
        ],
        compiler_params=pltpu.CompilerParams(
            collective_id=0, has_side_effects=True, vmem_limit_bytes=48 * 2**20
        ),
        cost_estimate=pl.CostEstimate(
            flops=16 * n * cap * units * features,
            bytes_accessed=12 * units * features + 6 * rows * width,
            transcendentals=n * cap * units,
        ),
    )(partner, token_expert.reshape(1, rows), tokens, cotangent, gate_weight, up_weight, down_weight)


def body(tokens, cotangent, token_expert, partner, gate_weight, up_weight, down_weight):
    n, ranks = lax.axis_size("ep"), lax.axis_size("tp")
    rows, width = tokens.shape
    cap = capacity_of(rows, n)
    tiled = cap % 16 == 0 and rows % 128 == 0 and width % 128 == 0 and n % 2 == 0 and ranks == 4
    fits = 32 * n * cap * width <= 8 * 2**20
    chosen = kernel_body if tiled and fits else plain_body
    return chosen(tokens, cotangent, token_expert, partner, gate_weight, up_weight, down_weight)


def solution(mesh):
    in_specs = (
        P("ep", "tp"),
        P("ep", "tp"),
        P("ep"),
        P(),
        P("ep", "tp", None),
        P("ep", "tp", None),
        P("ep", "tp", None),
    )
    out_specs = (P("ep", "tp"), P("ep", "tp", None), P("ep", "tp", None), P("ep", "tp", None))
    return jax.shard_map(body, mesh=mesh, in_specs=in_specs, out_specs=out_specs, check_vma=False)
```

profile of v0, /device:TPU:19, one launch (start us, length us, event | category | flops | bytes accessed | tf_op | source)
XLA Modules:
  0.0 76.2 jit_solution(8034475920162547634)
XLA Ops:
  0.6 0.0 copy-start.5
  0.6 0.0 copy-start.6
  0.7 0.6 copy-done.5
  1.3 0.0 copy-done.6
  1.3 0.0 copy-start
  1.3 1.1 %copy-done = bf16[1,192,2048]{2,1,0:T(8,128)(2,1)S(1)} copy-done((bf16[1,192,2048]{2,1,0:T(8,128)(2,1)S(1)}, bf16[1,192,2048]{2,1,0:T(8,128)(2,1)}, u32[]{:S(2)}) %copy-start) | copy-done | bytes 786456
  2.4 0.0 copy-start.1
  2.4 1.1 %copy-done.1 = bf16[1,192,2048]{2,1,0:T(8,128)(2,1)S(1)} copy-done((bf16[1,192,2048]{2,1,0:T(8,128)(2,1)S(1)}, bf16[1,192,2048]{2,1,0:T(8,128)(2,1)}, u32[]{:S(2)}) %copy-start.1) | copy-done | bytes 786456
  3.6 0.0 copy-start.2
  3.6 1.1 %copy-done.2 = bf16[1,192,2048]{2,1,0:T(8,128)(2,1)S(1)} copy-done((bf16[1,192,2048]{2,1,0:T(8,128)(2,1)S(1)}, bf16[1,192,2048]{2,1,0:T(8,128)(2,1)}, u32[]{:S(2)}) %copy-start.2) | copy-done | bytes 786456
  4.7 0.0 copy-start.3
  4.7 0.9 %copy-done.3 = bf16[128,512]{1,0:T(8,128)(2,1)S(1)} copy-done((bf16[128,512]{1,0:T(8,128)(2,1)S(1)}, bf16[128,512]{1,0:T(8,128)(2,1)}, u32[]{:S(2)}) %copy-start.3) | copy-done | bytes 131096
  5.6 0.0 copy-start.4
  5.6 0.9 %copy-done.4 = bf16[128,512]{1,0:T(8,128)(2,1)S(1)} copy-done((bf16[128,512]{1,0:T(8,128)(2,1)S(1)}, bf16[128,512]{1,0:T(8,128)(2,1)}, u32[]{:S(2)}) %copy-start.4) | copy-done | bytes 131096
  6.5 66.4 %shard_map.102 = (bf16[128,512]{1,0:T(8,128)(2,1)S(1)}, bf16[1,192,2048]{2,1,0:T(8,128)(2,1)S(1)}, bf16[1,192,2048]{2,1,0:T(8,128)(2,1)S(1)}, bf16[1,192,2048]{2,1,0:T(8,128)(2,1)S(1)}) custom-call(s32[8]{0:T(128)S(1)} %copy-done.5, s32[1,128]{1,0:T(1,128)S(1)} %bitcast.1, bf16[128,512]{1,0:T(8,128)(2,1)S(1)} %copy-done.3, bf16[128,512]{1,0:T(8,128)(2,1)S(1)} %copy-done.4, ...), custom_call_target="tpu_custom_call" | custom-call | flops 1610612736 | bytes 5111808 | tf_op jit(solution)/shard_map/pallas_call | solution.py:324
  72.9 0.7 copy.15
  73.6 0.9 %copy.16 = bf16[1,192,2048]{2,1,0:T(8,128)(2,1)} copy(bf16[1,192,2048]{2,1,0:T(8,128)(2,1)S(1)} %get-tuple-element.9) | data formatting | bytes 1572864
  74.5 0.9 %copy.17 = bf16[1,192,2048]{2,1,0:T(8,128)(2,1)} copy(bf16[1,192,2048]{2,1,0:T(8,128)(2,1)S(1)} %get-tuple-element.10) | data formatting | bytes 1572864
  75.3 0.9 %copy.18 = bf16[1,192,2048]{2,1,0:T(8,128)(2,1)} copy(bf16[1,192,2048]{2,1,0:T(8,128)(2,1)S(1)} %get-tuple-element.11) | data formatting | bytes 1572864
Async XLA Ops:
  0.6 0.7 copy-start.5
  0.6 0.7 copy-start.6
  1.3 1.1 %copy-start = (bf16[1,192,2048]{2,1,0:T(8,128)(2,1)S(1)}, bf16[1,192,2048]{2,1,0:T(8,128)(2,1)}, u32[]{:S(2)}) copy-start(bf16[1,192,2048]{2,1,0:T(8,128)(2,1)} %wg_in.1) | copy-start | bytes 2359300
  2.4 1.1 %copy-start.1 = (bf16[1,192,2048]{2,1,0:T(8,128)(2,1)S(1)}, bf16[1,192,2048]{2,1,0:T(8,128)(2,1)}, u32[]{:S(2)}) copy-start(bf16[1,192,2048]{2,1,0:T(8,128)(2,1)} %wu_in.1) | copy-start | bytes 2359300
  3.6 1.1 %copy-start.2 = (bf16[1,192,2048]{2,1,0:T(8,128)(2,1)S(1)}, bf16[1,192,2048]{2,1,0:T(8,128)(2,1)}, u32[]{:S(2)}) copy-start(bf16[1,192,2048]{2,1,0:T(8,128)(2,1)} %wd_in.1) | copy-start | bytes 2359300
  4.7 0.9 %copy-start.3 = (bf16[128,512]{1,0:T(8,128)(2,1)S(1)}, bf16[128,512]{1,0:T(8,128)(2,1)}, u32[]{:S(2)}) copy-start(bf16[128,512]{1,0:T(8,128)(2,1)} %tok.1) | copy-start | bytes 393220
  5.6 0.9 %copy-start.4 = (bf16[128,512]{1,0:T(8,128)(2,1)S(1)}, bf16[128,512]{1,0:T(8,128)(2,1)}, u32[]{:S(2)}) copy-start(bf16[128,512]{1,0:T(8,128)(2,1)} %cot.1) | copy-start | bytes 393220
where the time goes:
time: 76.5 us; the launch traced here: 76.2 us
  Pallas kernels  66.4 us (87%)
  local copies, waits for them, and re-layouts  9.16 us (12%)
    pallas_call x1, Pallas kernels, kernel_body(): pl.pallas_call(functools.partial(swap_kernel, n, cap, groups), out_shape=...  66.4 us
    unnamed x18, local copies, waits for them, and re-layouts  9.16 us

commit v1 on v0

--- a/solution.py
+++ b/solution.py
@@ -81,13 +81,57 @@
     )
 
 
+def slots_of(te, cap):
+    rows = te.shape[1]
+    te_lane = jnp.broadcast_to(te.astype(F32), (rows, rows))
+    te_sub = te_lane.T
+    at0 = lax.broadcasted_iota(jnp.int32, (rows, rows), 0)
+    at1 = lax.broadcasted_iota(jnp.int32, (rows, rows), 1)
+    same = te_lane == te_sub
+    pos_lane = jnp.sum(jnp.where(same & (at0 < at1), 1.0, 0.0), axis=0, keepdims=True)
+    pos_sub = jnp.sum(jnp.where(same & (at1 < at0), 1.0, 0.0), axis=1, keepdims=True)
+    return te.astype(F32) * float(cap) + pos_lane, pos_lane, te_sub[:, :1] * float(cap) + pos_sub
+
+
+WAVE, G0, BP = False, 0, 0
+
+
+def result_kernel(
+    cap, te, full_p, terms_p, ret, tg_out, gg_out, gu_out, gd_out, tg_v, g_v, out_sem
+):
+    n, _, padded = terms_p.shape
+    rows, width = tg_v.shape
+    units = g_v.shape[1]
+    slots = n * cap
+    turned = terms_p[...].reshape(slots, padded).astype(F32).T.astype(BF16)
+    copies = []
+    for q in range(4):
+        columns = pl.ds(q * width, width)
+        x_q = full_p[q, :, 0].reshape(slots, width)
+        g_q = full_p[q, :, 1].reshape(slots, width)
+        for i, (out, by) in enumerate(((gg_out, x_q), (gu_out, x_q), (gd_out, g_q))):
+            part = turned[i * units : (i + 1) * units]
+            g_v[3 * q + i] = jnp.dot(part, by, preferred_element_type=F32).astype(BF16)
+            copy = pltpu.make_async_copy(g_v.at[3 * q + i], out.at[0, :, columns], out_sem.at[3 * q + i])
+            copy.start()
+            copies.append(copy)
+    _, _, slot_sub = slots_of(te[...], cap)
+    across = lax.broadcasted_iota(jnp.int32, (rows, slots), 1).astype(F32)
+    home = jnp.where(across == slot_sub, 1.0, 0.0).astype(BF16)
+    tg_v[...] = jnp.dot(home, ret[...].reshape(slots, width), preferred_element_type=F32).astype(BF16)
+    copy = pltpu.make_async_copy(tg_v, tg_out, out_sem.at[12])
+    copy.start()
+    for done in copies + [copy]:
+        done.wait()
+
+
 def swap_kernel(
     n, cap, groups,
-    partner, te, tok, cot, wg_in, wu_in, wd_in,
-    tg_out, gg_out, gu_out, gd_out,
-    w_v, send_e, send_p, full_e, full_p, terms, mid, send2, terms_p,
-    keep, c1s, c1r, c2s, c2r, shares, ret,
-    w_sem, ae, ap, be, bp, e1, e2, c1, c2, dd,
+    partner, te, tok_in, cot_in, wg_in, wu_in, wd_in,
+    full_p, terms_p, ret,
+    tok, cot, w_v, send_e, send_p, full_e, terms, mid, send2,
+    keep, c1s, c1r, c2s, c2r, shares,
+    t_sem, w_sem, ae, ap, be, bp, e1, e2, c1, c2, dd,
 ):
     rows, width = tok.shape
     units = wg_in.shape[1]
@@ -97,9 +141,15 @@
     sib = t + 1 - 2 * lax.rem(t, 2)
     ctr = lax.rem(t + 2, 4)
     far = lax.rem(sib + 2, 4)
+    order = [i + j for i in range(n // 2) for j in (0, n // 2)]
     ahead = lambda k: lax.rem(me + k, n)
     behind = lambda k: lax.rem(me + n - k, n)
 
+    t_copies = [
+        pltpu.make_async_copy(a, v, t_sem.at[i]) for i, (a, v) in enumerate(((tok_in, tok), (cot_in, cot)))
+    ]
+    for copy in t_copies:
+        copy.start()
     barrier = pltpu.get_barrier_semaphore()
 
     def greet(k, carry):
@@ -120,18 +170,9 @@
     for copy in w_copies:
         copy.start()
 
-    te_lane = jnp.broadcast_to(te[...].astype(F32), (rows, rows))
-    te_sub = te_lane.T
-    at0 = lax.broadcasted_iota(jnp.int32, (rows, rows), 0)
-    at1 = lax.broadcasted_iota(jnp.int32, (rows, rows), 1)
-    same = te_lane == te_sub
-    pos_lane = jnp.sum(jnp.where(same & (at0 < at1), 1.0, 0.0), axis=0, keepdims=True)
-    pos_sub = jnp.sum(jnp.where(same & (at1 < at0), 1.0, 0.0), axis=1, keepdims=True)
-    slot_lane = te[...].astype(F32) * float(cap) + pos_lane
-    slot_sub = te_sub[:, :1] * float(cap) + pos_sub
+    slot_lane, pos_lane, _ = slots_of(te[...], cap)
     slots = n * cap
     down = lax.broadcasted_iota(jnp.int32, (slots, rows), 0).astype(F32)
-    across = lax.broadcasted_iota(jnp.int32, (rows, slots), 1).astype(F32)
 
     def pick(slot, send):
         hot = jnp.where(down == slot, 1.0, 0.0).astype(BF16)
@@ -139,13 +180,15 @@
             rows_of = jnp.dot(hot, source[...], preferred_element_type=F32).astype(BF16)
             send[:, i] = rows_of.reshape(n, cap, width)
 
-    def dispatch(send, full, sem):
-        def go(k, carry):
+    def dispatch(send, full, sem, ks):
+        for k in ks:
             to = ahead(k)
             remote(send.at[to], full.at[t, me], sem.at[0, to], sem.at[1, me], {"ep": to}).start()
-            return carry
-        lax.fori_loop(1, n, go, 0)
-        full[t, me] = send[me]
+
+    def sent(send, sem, ks):
+        for k in ks:
+            to = ahead(k)
+            remote(send.at[to], send.at[to], sem.at[0, to], sem.at[1, to], {"ep": to}).wait_send()
 
     def share_own(full, b, s):
         remote(full.at[t, s], full.at[t, s], b.at[1, s], b.at[4, s], {"tp": ctr}).start()
@@ -162,33 +205,40 @@
         remote(full.at[sib, s], full.at[sib, s], b.at[0, s], b.at[3, s], {"tp": sib}).wait_recv()
         remote(full.at[far, s], full.at[far, s], b.at[2, s], b.at[5, s], {"tp": sib}).wait_recv()
 
-    def spread(full, a, b):
-        share_own(full, b, me)
-
-        def step(k, carry):
+    def take(full, a, b, ks):
+        for k in ks:
             s = behind(k)
-            got_own(full, a, s, k)
+            if k:
+                got_own(full, a, s, k)
             share_own(full, b, s)
-            pass_on(full, b, behind(k - 1))
-            return carry
-        lax.fori_loop(1, n, step, 0)
-        pass_on(full, b, behind(n - 1))
-
+
+    def relay(full, b, ks):
+        for k in ks:
+            pass_on(full, b, behind(k))
+
+    half = n // groups
+    first, second = order[:half], order[half:]
+    for copy in t_copies:
+        copy.wait()
     pick(slot_lane, send_e)
     pl.semaphore_wait(barrier, n + 1)
-    dispatch(send_e, full_e, ae)
+    dispatch(send_e, full_e, ae, first[1:])
+    full_e[t, me] = send_e[me]
     moved = pos_lane
     for e in range(n):
         moved = moved + jnp.where(te[...] == e, (partner[e] * cap).astype(F32), 0.0)
     pick(moved, send_p)
-    spread(full_e, ae, be)
-    dispatch(send_p, full_p, ap)
-    for copy in w_copies:
-        copy.wait()
+    full_p[t, me] = send_p[me]
+    if WAVE:
+        sent(send_e, ae, first[1:])
+    dispatch(send_e, full_e, ae, second)
+    if not WAVE:
+        sent(send_e, ae, first[1:])
 
     slices = (t, ctr, sib, far)
-    for h in range(groups):
-        ks = range(h * per, (h + 1) * per)
+
+    def compute(h):
+        ks = order[h * per : (h + 1) * per]
         for k in ks:
             got_sibling(full_e, be, behind(k))
         gate = jnp.zeros((per * cap, units), F32)
@@ -208,6 +258,12 @@
             terms[behind(k), :, 2 * units : 3 * units] = hidden[cut]
             if terms.shape[2] > 3 * units:
                 terms[behind(k), :, 3 * units :] = jnp.zeros((cap, terms.shape[2] - 3 * units), BF16)
+        for k in ks:
+            s = behind(k)
+            if k == 0:
+                mid[me] = terms[me]
+            else:
+                remote(terms.at[s], mid.at[me], e1.at[0, s], e1.at[1, me], {"ep": s}).start()
         for i in (2, 3):
             q = slices[i]
             c1s[h, i - 2] = (
@@ -215,39 +271,76 @@
                 + jnp.dot(up_term, w_v[1, q], preferred_element_type=F32)
             ).astype(BF16)
         remote(c1s.at[h], c1r.at[h], c1.at[0, h], c1.at[1, h], {"tp": sib}).start()
-        for k in ks:
-            s = behind(k)
-            if k == 0:
-                mid[me] = terms[me]
-            else:
-                remote(terms.at[s], mid.at[me], e1.at[0, s], e1.at[1, me], {"ep": s}).start()
         for i in (0, 1):
             q = slices[i]
             keep[h, i] = jnp.dot(gate_term, w_v[0, q], preferred_element_type=F32) + jnp.dot(
                 up_term, w_v[1, q], preferred_element_type=F32
             )
 
-    for h in range(groups):
+    def sum_siblings(h):
         remote(c1s.at[h], c1r.at[h], c1.at[0, h], c1.at[1, h], {"tp": sib}).wait_recv()
         c2s[h] = (keep[h, 1] + c1r[h, 1].astype(F32)).astype(BF16)
         remote(c2s.at[h], c2r.at[h], c2.at[0, h], c2.at[1, h], {"tp": ctr}).start()
 
+    def send_back(h):
+        remote(c2s.at[h], c2r.at[h], c2.at[0, h], c2.at[1, h], {"tp": ctr}).wait_recv()
+        total = (keep[h, 0] + c1r[h, 0].astype(F32) + c2r[h].astype(F32)).astype(BF16)
+        shares[h * per : (h + 1) * per] = total.reshape(per, cap, width)
+        for i in range(h * per, (h + 1) * per):
+            s = behind(order[i])
+            if i == 0:
+                ret[me] = shares[0]
+            else:
+                remote(shares.at[i], ret.at[me], dd.at[0, s], dd.at[1, me], {"ep": s}).start()
+
+    def weights_ready():
+        for copy in w_copies:
+            copy.wait()
+
+    take(full_e, ae, be, first)
+    relay(full_e, be, first)
+    weights_ready()
+    if G0:
+        compute(0)
+        take(full_e, ae, be, second)
+        dispatch(send_p, full_p, ap, order[1:])
+    else:
+        take(full_e, ae, be, second)
+        dispatch(send_p, full_p, ap, order[1:])
+        compute(0)
+    sum_siblings(0)
+    relay(full_e, be, second)
+    if BP == 0:
+        compute(1)
+        send_back(0)
+        sum_siblings(1)
+        take(full_p, ap, bp, order)
+        send_back(1)
+    elif BP == 1:
+        compute(1)
+        send_back(0)
+        sum_siblings(1)
+        send_back(1)
+        take(full_p, ap, bp, order)
+    elif BP == 2:
+        send_back(0)
+        compute(1)
+        sum_siblings(1)
+        take(full_p, ap, bp, order)
+        send_back(1)
+    elif BP == 3:
+        compute(1)
+        send_back(0)
+        sum_siblings(1)
+        take(full_p, ap, bp, first)
+        send_back(1)
+        take(full_p, ap, bp, second)
+
     def first_hop(k, carry):
         s = ahead(k)
         remote(mid.at[s], mid.at[s], e1.at[0, s], e1.at[1, s], {"ep": s}).wait_recv()
         return carry
     lax.fori_loop(1, n, first_hop, 0)
-
-    for h in range(groups):
-        remote(c2s.at[h], c2r.at[h], c2.at[0, h], c2.at[1, h], {"tp": ctr}).wait_recv()
-        total = (keep[h, 0] + c1r[h, 0].astype(F32) + c2r[h].astype(F32)).astype(BF16)
-        shares[h * per : (h + 1) * per] = total.reshape(per, cap, width)
-        for k in range(h * per, (h + 1) * per):
-            s = behind(k)
-            if k == 0:
-                ret[me] = shares[0]
-            else:
-                remote(shares.at[k], ret.at[me], dd.at[0, s], dd.at[1, me], {"ep": s}).start()
 
     def second_hop(k, carry):
         d = ahead(k)
@@ -256,41 +349,24 @@
         return carry
     lax.fori_loop(1, n, second_hop, 0)
     terms_p[me] = mid[partner[me]]
-
-    spread(full_p, ap, bp)
+    relay(full_p, bp, order)
 
     def returned(k, carry):
         s = behind(k)
         remote(ret.at[s], ret.at[s], dd.at[0, s], dd.at[1, s], {"ep": s}).wait_recv()
+        remote(terms_p.at[s], terms_p.at[s], e2.at[0, s], e2.at[1, s], {"ep": s}).wait_recv()
         return carry
     lax.fori_loop(1, n, returned, 0)
-    home = jnp.where(across == slot_sub, 1.0, 0.0).astype(BF16)
-    tg_out[...] = jnp.dot(home, ret[...].reshape(slots, width), preferred_element_type=F32).astype(BF16)
-
-    def arrived(k, carry):
-        s = behind(k)
-        remote(terms_p.at[s], terms_p.at[s], e2.at[0, s], e2.at[1, s], {"ep": s}).wait_recv()
-        return carry
-    lax.fori_loop(1, n, arrived, 0)
 
     def gathered(k, carry):
         got_sibling(full_p, bp, behind(k))
         return carry
     lax.fori_loop(0, n, gathered, 0)
 
-    flat = terms_p[...].reshape(slots, terms_p.shape[2])
-    turned = flat.astype(F32).T.astype(BF16)
-    for q in range(4):
-        columns = slice(q * width, (q + 1) * width)
-        x_q = full_p[q, :, 0].reshape(slots, width)
-        g_q = full_p[q, :, 1].reshape(slots, width)
-        gg_out[0, :, columns] = jnp.dot(turned[:units], x_q, preferred_element_type=F32).astype(BF16)
-        gu_out[0, :, columns] = jnp.dot(turned[units : 2 * units], x_q, preferred_element_type=F32).astype(BF16)
-        gd_out[0, :, columns] = jnp.dot(turned[2 * units : 3 * units], g_q, preferred_element_type=F32).astype(BF16)
+    sent(send_e, ae, second)
 
     def drain(k, carry):
         s = ahead(k)
-        remote(send_e.at[s], send_e.at[s], ae.at[0, s], ae.at[1, s], {"ep": s}).wait_send()
         remote(send_p.at[s], send_p.at[s], ap.at[0, s], ap.at[1, s], {"ep": s}).wait_send()
         remote(terms.at[s], terms.at[s], e1.at[0, s], e1.at[1, s], {"ep": s}).wait_send()
         remote(send2.at[s], send2.at[s], e2.at[0, s], e2.at[1, s], {"ep": s}).wait_send()
@@ -319,20 +395,29 @@
     padded = -(-3 * units // 128) * 128
     dma = pltpu.SemaphoreType.DMA
     vmem = pl.BlockSpec(memory_space=pltpu.VMEM)
-    anywhere = pl.BlockSpec(memory_space=pl.ANY)
+    hbm = pl.BlockSpec(memory_space=pltpu.HBM)
     grad = jax.ShapeDtypeStruct((1, units, features), BF16)
-    return pl.pallas_call(
+    te = token_expert.reshape(1, rows)
+    in_hbm = [
+        pltpu.with_memory_space_constraint(a, pltpu.HBM)
+        for a in (tokens, cotangent, gate_weight, up_weight, down_weight)
+    ]
+    kept, terms, back = pl.pallas_call(
         functools.partial(swap_kernel, n, cap, groups),
-        out_shape=(jax.ShapeDtypeStruct((rows, width), BF16), grad, grad, grad),
-        in_specs=[pl.BlockSpec(memory_space=pltpu.SMEM), vmem, vmem, vmem, anywhere, anywhere, anywhere],
-        out_specs=(vmem, vmem, vmem, vmem),
+        out_shape=(
+            jax.ShapeDtypeStruct((4, n, 2, cap, width), BF16),
+            jax.ShapeDtypeStruct((n, cap, padded), BF16),
+            jax.ShapeDtypeStruct((n, cap, width), BF16),
+        ),
+        in_specs=[pl.BlockSpec(memory_space=pltpu.SMEM), vmem] + [hbm] * 5,
+        out_specs=(vmem, vmem, vmem),
         scratch_shapes=[
+            pltpu.VMEM((rows, width), BF16),
+            pltpu.VMEM((rows, width), BF16),
             pltpu.VMEM((3, 4, units, width), BF16),
             pltpu.VMEM((n, 2, cap, width), BF16),
             pltpu.VMEM((n, 2, cap, width), BF16),
             pltpu.VMEM((4, n, 2, cap, width), BF16),
-            pltpu.VMEM((4, n, 2, cap, width), BF16),
-            pltpu.VMEM((n, cap, padded), BF16),
             pltpu.VMEM((n, cap, padded), BF16),
             pltpu.VMEM((n, cap, padded), BF16),
             pltpu.VMEM((n, cap, padded), BF16),
@@ -342,7 +427,7 @@
             pltpu.VMEM((groups, per * cap, width), BF16),
             pltpu.VMEM((groups, per * cap, width), BF16),
             pltpu.VMEM((n, cap, width), BF16),
-            pltpu.VMEM((n, cap, width), BF16),
+            dma((2,)),
             dma((3, 4)),
             dma((2, n)),
             dma((2, n)),
@@ -358,11 +443,28 @@
             collective_id=0, has_side_effects=True, vmem_limit_bytes=48 * 2**20
         ),
         cost_estimate=pl.CostEstimate(
-            flops=16 * n * cap * units * features,
-            bytes_accessed=12 * units * features + 6 * rows * width,
+            flops=10 * n * cap * units * features,
+            bytes_accessed=6 * units * features + 4 * rows * width,
             transcendentals=n * cap * units,
         ),
-    )(partner, token_expert.reshape(1, rows), tokens, cotangent, gate_weight, up_weight, down_weight)
+    )(partner, te, *in_hbm)
+    return pl.pallas_call(
+        functools.partial(result_kernel, cap),
+        out_shape=(jax.ShapeDtypeStruct((rows, width), BF16), grad, grad, grad),
+        in_specs=[vmem] * 4,
+        out_specs=(hbm,) * 4,
+        scratch_shapes=[
+            pltpu.VMEM((rows, width), BF16),
+            pltpu.VMEM((12, units, width), BF16),
+            dma((13,)),
+        ],
+        compiler_params=pltpu.CompilerParams(vmem_limit_bytes=32 * 2**20),
+        cost_estimate=pl.CostEstimate(
+            flops=6 * n * cap * units * features,
+            bytes_accessed=6 * units * features + 2 * rows * width,
+            transcendentals=0,
+        ),
+    )(te, kept, terms, back)
 
 
 def body(tokens, cotangent, token_expert, partner, gate_weight, up_weight, down_weight):

time: 76.5 us -> 56.3 us (0.74)
  the two profiles are of different devices: /device:TPU:19 before, /device:TPU:0 now
where the time goes in v1:
time: 56.3 us; the launch traced here: 56.1 us
  Pallas kernels  54.1 us (96%)
  local copies, waits for them, and re-layouts  1.3 us (2%)
  between operations  0.65 us (1%)
    pallas_call x1, Pallas kernels, kernel_body(): pl.pallas_call(functools.partial(swap_kernel, n, cap, groups), out_shape=...  52.3 us
    pallas_call x1, Pallas kernels, kernel_body(): pl.pallas_call(functools.partial(result_kernel, cap), out_shape=(jax.Shap...  1.81 us
    unnamed x4, local copies, waits for them, and re-layouts  1.3 us

profile of v1, /device:TPU:0, one launch (start us, length us, event | category | flops | bytes accessed | tf_op | source)
XLA Modules:
  0.0 56.1 jit_solution(17907231390053498250)
XLA Ops:
  0.6 0.0 copy-start
  0.6 0.6 %copy-done = s32[128]{0:T(128)S(1)} copy-done((s32[128]{0:T(128)S(1)}, s32[128]{0:T(128)}, u32[]{:S(2)}) %copy-start) | copy-done | bytes 536
  1.3 0.0 copy-start.1
  1.3 0.7 %copy-done.1 = s32[8]{0:T(128)S(1)} copy-done((s32[8]{0:T(128)S(1)}, s32[8]{0:T(128)}, u32[]{:S(2)}) %copy-start.1) | copy-done | bytes 56
  1.9 52.3 %shard_map.102 = (bf16[4,8,2,32,512]{4,3,2,1,0:T(8,128)(2,1)S(1)}, bf16[8,32,640]{2,1,0:T(8,128)(2,1)S(1)}, bf16[8,32,512]{2,1,0:T(8,128)(2,1)S(1)}) custom-call(s32[8]{0:T(128)S(1)} %copy-done.1, s32[1,128]{1,0:T(1,128)S(1)} %bitcast.1, bf16[128,512]{1,0:T(8,128)(2,1)} %tok_in.1, bf16[128,512]{1,0:T(8,128)(2,1)} %cot_in.1, bf16[1,192,2048]{2,1,0:T(8,128)(2,1)} %wg_in.1, ...), custom_call_target="tpu_custom_call" | custom-call | flops 1006632960 | bytes 2621440 | tf_op jit(solution)/shard_map/pallas_call | solution.py:405
  54.3 1.8 %shard_map.103 = (bf16[128,512]{1,0:T(8,128)(2,1)}, bf16[1,192,2048]{2,1,0:T(8,128)(2,1)}, bf16[1,192,2048]{2,1,0:T(8,128)(2,1)}, bf16[1,192,2048]{2,1,0:T(8,128)(2,1)}) custom-call(s32[1,128]{1,0:T(1,128)S(1)} %bitcast.2, bf16[4,8,2,32,512]{4,3,2,1,0:T(8,128)(2,1)S(1)} %get-tuple-element.7.full_p, bf16[8,32,640]{2,1,0:T(8,128)(2,1)S(1)} %get-tuple-element.8.terms_p, ...), custom_call_target="tpu_custom_call" | custom-call | flops 603979776 | bytes 2490368 | tf_op jit(solution)/shard_map/pallas_call | solution.py:451
Async XLA Ops:
  0.6 0.7 %copy-start = (s32[128]{0:T(128)S(1)}, s32[128]{0:T(128)}, u32[]{:S(2)}) copy-start(s32[128]{0:T(128)} %param.9) | copy-start | bytes 1540
  1.3 0.7 %copy-start.1 = (s32[8]{0:T(128)S(1)}, s32[8]{0:T(128)}, u32[]{:S(2)}) copy-start(s32[8]{0:T(128)} %partner.1) | copy-start | bytes 100

commit v2 on v1

--- a/solution.py
+++ b/solution.py
@@ -93,7 +93,7 @@
     return te.astype(F32) * float(cap) + pos_lane, pos_lane, te_sub[:, :1] * float(cap) + pos_sub
 
 
-WAVE, G0, BP = False, 0, 0
+WAVE, G0, BP = False, 0, 2
 
 
 def result_kernel(
@@ -127,9 +127,9 @@
 
 def swap_kernel(
     n, cap, groups,
-    partner, te, tok_in, cot_in, wg_in, wu_in, wd_in,
+    partner_in, te_in, tok_in, cot_in, wg_in, wu_in, wd_in,
     full_p, terms_p, ret,
-    tok, cot, w_v, send_e, send_p, full_e, terms, mid, send2,
+    partner, te, tok, cot, w_v, send_e, send_p, full_e, terms, mid, send2,
     keep, c1s, c1r, c2s, c2r, shares,
     t_sem, w_sem, ae, ap, be, bp, e1, e2, c1, c2, dd,
 ):
@@ -146,7 +146,7 @@
     behind = lambda k: lax.rem(me + n - k, n)
 
     t_copies = [
-        pltpu.make_async_copy(a, v, t_sem.at[i]) for i, (a, v) in enumerate(((tok_in, tok), (cot_in, cot)))
+        pltpu.make_async_copy(a, v, t_sem.at[i]) for i, (a, v) in enumerate(((te_in, te), (partner_in, partner), (tok_in, tok), (cot_in, cot)))
     ]
     for copy in t_copies:
         copy.start()
@@ -170,6 +170,8 @@
     for copy in w_copies:
         copy.start()
 
+    for copy in t_copies:
+        copy.wait()
     slot_lane, pos_lane, _ = slots_of(te[...], cap)
     slots = n * cap
     down = lax.broadcasted_iota(jnp.int32, (slots, rows), 0).astype(F32)
@@ -218,8 +220,6 @@
 
     half = n // groups
     first, second = order[:half], order[half:]
-    for copy in t_copies:
-        copy.wait()
     pick(slot_lane, send_e)
     pl.semaphore_wait(barrier, n + 1)
     dispatch(send_e, full_e, ae, first[1:])
@@ -298,19 +298,39 @@
             copy.wait()
 
     take(full_e, ae, be, first)
-    relay(full_e, be, first)
+    if G0 != 0:
+        relay(full_e, be, first)
     weights_ready()
-    if G0:
+    if G0 == 1:
         compute(0)
         take(full_e, ae, be, second)
         dispatch(send_p, full_p, ap, order[1:])
-    else:
+    elif G0 == 0:
         take(full_e, ae, be, second)
         dispatch(send_p, full_p, ap, order[1:])
+        relay(full_e, be, first)
+        compute(0)
+    else:
+        dispatch(send_p, full_p, ap, first[1:])
+        take(full_e, ae, be, second)
+        dispatch(send_p, full_p, ap, second)
         compute(0)
     sum_siblings(0)
     relay(full_e, be, second)
-    if BP == 0:
+    if BP == 6:
+        take(full_p, ap, bp, first)
+        compute(1)
+        send_back(0)
+        sum_siblings(1)
+        take(full_p, ap, bp, second)
+        send_back(1)
+    elif BP == 7:
+        compute(1)
+        take(full_p, ap, bp, order)
+        send_back(0)
+        sum_siblings(1)
+        send_back(1)
+    elif BP == 0:
         compute(1)
         send_back(0)
         sum_siblings(1)
@@ -335,12 +355,19 @@
         take(full_p, ap, bp, first)
         send_back(1)
         take(full_p, ap, bp, second)
+    else:
+        compute(1)
+        send_back(0)
+        sum_siblings(1)
+        send_back(1)
 
     def first_hop(k, carry):
         s = ahead(k)
         remote(mid.at[s], mid.at[s], e1.at[0, s], e1.at[1, s], {"ep": s}).wait_recv()
         return carry
     lax.fori_loop(1, n, first_hop, 0)
+    if BP == 5:
+        take(full_p, ap, bp, order)
 
     def second_hop(k, carry):
         d = ahead(k)
@@ -349,6 +376,8 @@
         return carry
     lax.fori_loop(1, n, second_hop, 0)
     terms_p[me] = mid[partner[me]]
+    if BP == 4:
+        take(full_p, ap, bp, order)
     relay(full_p, bp, order)
 
     def returned(k, carry):
@@ -400,7 +429,7 @@
     te = token_expert.reshape(1, rows)
     in_hbm = [
         pltpu.with_memory_space_constraint(a, pltpu.HBM)
-        for a in (tokens, cotangent, gate_weight, up_weight, down_weight)
+        for a in (partner, te, tokens, cotangent, gate_weight, up_weight, down_weight)
     ]
     kept, terms, back = pl.pallas_call(
         functools.partial(swap_kernel, n, cap, groups),
@@ -409,9 +438,11 @@
             jax.ShapeDtypeStruct((n, cap, padded), BF16),
             jax.ShapeDtypeStruct((n, cap, width), BF16),
         ),
-        in_specs=[pl.BlockSpec(memory_space=pltpu.SMEM), vmem] + [hbm] * 5,
+        in_specs=[hbm] * 7,
         out_specs=(vmem, vmem, vmem),
         scratch_shapes=[
+            pltpu.SMEM((n,), jnp.int32),
+            pltpu.VMEM((1, rows), jnp.int32),
             pltpu.VMEM((rows, width), BF16),
             pltpu.VMEM((rows, width), BF16),
             pltpu.VMEM((3, 4, units, width), BF16),
@@ -427,7 +458,7 @@
             pltpu.VMEM((groups, per * cap, width), BF16),
             pltpu.VMEM((groups, per * cap, width), BF16),
             pltpu.VMEM((n, cap, width), BF16),
-            dma((2,)),
+            dma((4,)),
             dma((3, 4)),
             dma((2, n)),
             dma((2, n)),
@@ -447,7 +478,7 @@
             bytes_accessed=6 * units * features + 4 * rows * width,
             transcendentals=n * cap * units,
         ),
-    )(partner, te, *in_hbm)
+    )(*in_hbm)
     return pl.pallas_call(
         functools.partial(result_kernel, cap),
         out_shape=(jax.ShapeDtypeStruct((rows, width), BF16), grad, grad, grad),

time: 56.3 us -> 52.7 us (0.936)
  Pallas kernels: 54.1 us -> 51.9 us
  local copies, waits for them, and re-layouts: 1.3 us -> 0.01 us
    pallas_call x1, Pallas kernels: 52.3 us -> 50.1 us  [kernel_body(): pl.pallas_call(functools.partial(swap_kernel, n, cap, groups), out_shape=...]
    unnamed x4 -> x2, local copies, waits for them, and re-layouts: 1.3 us -> 0.01 us
where the time goes in v2:
time: 52.7 us; the launch traced here: 52.5 us
  Pallas kernels  51.9 us (98%)
  between operations  0.66 us (1%)
    pallas_call x1, Pallas kernels, kernel_body(): pl.pallas_call(functools.partial(swap_kernel, n, cap, groups), out_shape=...  50.1 us
    pallas_call x1, Pallas kernels, kernel_body(): pl.pallas_call(functools.partial(result_kernel, cap), out_shape=(jax.Shap...  1.82 us

profile of v2, /device:TPU:0, one launch (start us, length us, event | category | flops | bytes accessed | tf_op | source)
XLA Modules:
  0.0 52.5 jit_solution(2088306205690642092)
XLA Ops:
  0.6 0.0 copy-start
  0.6 50.1 %shard_map.102 = (bf16[4,8,2,32,512]{4,3,2,1,0:T(8,128)(2,1)S(1)}, bf16[8,32,640]{2,1,0:T(8,128)(2,1)S(1)}, bf16[8,32,512]{2,1,0:T(8,128)(2,1)S(1)}) custom-call(s32[8]{0:T(128)} %partner_in.1, s32[1,128]{1,0:T(1,128)} %bitcast.1, bf16[128,512]{1,0:T(8,128)(2,1)} %tok_in.1, bf16[128,512]{1,0:T(8,128)(2,1)} %cot_in.1, bf16[1,192,2048]{2,1,0:T(8,128)(2,1)} %wg_in.1, ...), custom_call_target="tpu_custom_call" | custom-call | flops 1006632960 | bytes 2621440 | tf_op jit(solution)/shard_map/pallas_call | solution.py:434
  50.7 0.0 copy-done
  50.7 1.8 %shard_map.103 = (bf16[128,512]{1,0:T(8,128)(2,1)}, bf16[1,192,2048]{2,1,0:T(8,128)(2,1)}, bf16[1,192,2048]{2,1,0:T(8,128)(2,1)}, bf16[1,192,2048]{2,1,0:T(8,128)(2,1)}) custom-call(s32[1,128]{1,0:T(1,128)S(1)} %bitcast.2, bf16[4,8,2,32,512]{4,3,2,1,0:T(8,128)(2,1)S(1)} %get-tuple-element.7.full_p, bf16[8,32,640]{2,1,0:T(8,128)(2,1)S(1)} %get-tuple-element.8.terms_p, ...), custom_call_target="tpu_custom_call" | custom-call | flops 603979776 | bytes 2490368 | tf_op jit(solution)/shard_map/pallas_call | solution.py:482
Async XLA Ops:
  0.6 50.1 %copy-start = (s32[128]{0:T(128)S(1)}, s32[128]{0:T(128)}, u32[]{:S(2)}) copy-start(s32[128]{0:T(128)} %param.9) | copy-start | bytes 1540
